TPU v7x, 32 devices: a whole 2x2x4 slice. The times are simulated.
32 devices in a mesh: ctx: 16 (over z, x, core), exp: 2 (over y).
Axes of the slice: x: 2, y: 2, z: 4, core: 2. Of those that a mesh axis runs over, the one named last changes fastest.
Arguments:
- hidden: bfloat16 [4096, 2048], P(('ctx', 'exp')), may hold values from -1.5 to 1.5
- lengths: int32 [2], replicated, may hold values from 1024 to 2048, as said below
- routes: int32 [4096, 8], P(('ctx', 'exp')), may hold values from 0 to 127, all different within a row; in each aligned block of 128 rows (0 to 127, 128 to 255, ...) at most 16 rows name the same one
- gates: float32 [4096, 8], P(('ctx', 'exp')), may hold values from 0.05 to 0.5
- attn_gain: float32 [2048], replicated, may hold values from 0.25 to 1.75
- q_weight: bfloat16 [2048, 4096], P('ctx', 'exp'), may hold values from -0.125 to 0.125
- key_value_weight: bfloat16 [2048, 1024], P('ctx'), may hold values from -0.125 to 0.125
- q_gain: float32 [128], replicated, may hold values from 0.25 to 1.75
- k_gain: float32 [128], replicated, may hold values from 0.25 to 1.75
- o_weight: bfloat16 [4096, 2048], P('exp', 'ctx'), may hold values from -0.09375 to 0.09375
- moe_gain: float32 [2048], replicated, may hold values from 0.25 to 1.75
- expert_in: bfloat16 [128, 2048, 1536], P(('ctx', 'exp')), may hold values from -0.125 to 0.125
- expert_out: bfloat16 [128, 768, 2048], P(('ctx', 'exp')), may hold values from -0.21875 to 0.21875
Outputs:
- new_hidden: bfloat16 [4096, 2048], P(('ctx', 'exp'))
- cache: bfloat16 [2, 4096, 512], P(None, 'ctx', 'exp')
Inputs may be any that keep to these rules, and one draw needn't show every extreme that they name: `lengths`: one of the two prompts has exactly 2048 positions; the other has 1024 to 2048. `routes`: A row names 8 different experts. Within the 128 rows of each device (aligned blocks of rows) no expert is named more than 16 times, a bound that some block reaches.
All inputs are finite; a program needn't handle non-finite values.
Results may differ from a plain program's by a relative error of at most 0.02.
Values may be sent and summed in bfloat16 or wider, within the bound.
A program may use at most 128 MiB of HBM per device.

v0:
```python
import jax
import jax.numpy as jnp
from jax import lax
from jax.sharding import PartitionSpec as P

MODEL_WIDTH = 2048
QUERY_HEADS = 32
KEY_VALUE_HEADS = 4
HEAD_SIZE = 128
EXPERTS = 128
TOP = 8


epsilon = 1e-06
rope_base = 1000000.0


def from_behind(block, axis, distance):
    devices = range(lax.axis_size(axis))
    route = [((i - distance) % len(devices), i) for i in devices]
    return lax.ppermute(block, axis, route)


def rms_scale(values, gain):
    mean_square = jnp.mean(values * values, axis=-1, keepdims=True)
    return values * lax.rsqrt(mean_square + epsilon) * gain


def mirrored_position(row_ids, count_ctx, tok_ctx):
    half_rows = tok_ctx // 2
    holder = row_ids // tok_ctx
    within = row_ids % tok_ctx
    block_no = jnp.where(within < half_rows, holder, 2 * count_ctx - 1 - holder)
    return block_no * half_rows + within % half_rows


def document_info(token_positions, lengths):
    first_end = lengths[0]
    second_end = lengths[0] + lengths[1]
    document = (token_positions >= first_end).astype(jnp.int32) + (
        token_positions >= second_end
    ).astype(jnp.int32)
    doc_start = jnp.where(document == 0, 0, jnp.where(document == 1, first_end, second_end))
    return (document, token_positions - doc_start)


def rotate(values, rope_pos):
    head_width = values.shape[-1]
    freq_ids = jnp.arange(head_width // 2, dtype=jnp.float32)
    inverse = rope_base ** (-2.0 * freq_ids / head_width)
    angles = rope_pos.astype(jnp.float32)[:, None] * inverse[None, :]
    cosine = jnp.cos(angles)[:, None, :]
    sine_part = jnp.sin(angles)[:, None, :]
    first_half = values[..., : head_width // 2]
    second_half = values[..., head_width // 2 :]
    return jnp.concatenate(
        [
            first_half * cosine - second_half * sine_part,
            second_half * cosine + first_half * sine_part,
        ],
        axis=-1,
    )


def shards(
    hidden,
    lengths,
    routes,
    gates,
    attn_gain,
    q_weight,
    key_value_weight,
    q_gain,
    k_gain,
    o_weight,
    moe_gain,
    expert_in,
    expert_out,
):
    count_ctx = lax.axis_size("ctx")
    expert_count = lax.axis_size("exp")
    my_ctx = lax.axis_index("ctx")
    my_exp = lax.axis_index("exp")
    tok_dev = hidden.shape[0]
    tok_ctx = tok_dev * expert_count
    half_rows = tok_ctx // 2
    head_groups = QUERY_HEADS // KEY_VALUE_HEADS
    q_dev = QUERY_HEADS // expert_count
    key_value_share = max(1, KEY_VALUE_HEADS // expert_count)
    group_dev = q_dev // key_value_share
    column_share = KEY_VALUE_HEADS * HEAD_SIZE // expert_count
    key_value_leading = my_exp * q_dev // head_groups
    col_offset = my_exp * column_share - key_value_leading * HEAD_SIZE
    score_scale = HEAD_SIZE ** (-0.5)
    query_pos = mirrored_position(
        my_ctx * tok_ctx + jnp.arange(tok_ctx, dtype=jnp.int32), count_ctx, tok_ctx
    )
    query_doc, query_rope = document_info(query_pos, lengths)
    normed_own = rms_scale(hidden.astype(jnp.float32), attn_gain).astype(jnp.bfloat16)
    normed = lax.all_gather(normed_own, "exp", axis=0, tiled=True)
    key_cols = lax.dynamic_slice_in_dim(
        key_value_weight, key_value_leading * HEAD_SIZE, key_value_share * HEAD_SIZE, 1
    )
    value_column_block = lax.dynamic_slice_in_dim(
        key_value_weight,
        KEY_VALUE_HEADS * HEAD_SIZE + key_value_leading * HEAD_SIZE,
        key_value_share * HEAD_SIZE,
        1,
    )
    kv_local = jnp.concatenate([key_cols, value_column_block], axis=1)
    q_raw = jnp.dot(
        normed,
        lax.all_gather(q_weight, "ctx", axis=0, tiled=True),
        preferred_element_type=jnp.float32,
    )
    key_value_plain = jnp.dot(
        normed,
        lax.all_gather(kv_local, "ctx", axis=0, tiled=True),
        preferred_element_type=jnp.float32,
    )
    queries = rotate(
        rms_scale(q_raw.reshape(tok_ctx, q_dev, HEAD_SIZE), q_gain), query_rope
    ).astype(jnp.bfloat16)
    key_row_block = rotate(
        rms_scale(
            key_value_plain[:, : key_value_share * HEAD_SIZE].reshape(
                tok_ctx, key_value_share, HEAD_SIZE
            ),
            k_gain,
        ),
        query_rope,
    ).astype(jnp.bfloat16)
    value_row_block = key_value_plain[:, key_value_share * HEAD_SIZE :].astype(jnp.bfloat16)
    key_values = jnp.stack(
        [key_row_block.reshape(tok_ctx, key_value_share * HEAD_SIZE), value_row_block]
    )
    query_groups = queries.reshape(tok_ctx, key_value_share, group_dev, HEAD_SIZE)

    def attend(state_now, block_kv, offset):
        length_now = block_kv.shape[1]
        key_pos = mirrored_position(
            offset + jnp.arange(length_now, dtype=jnp.int32), count_ctx, tok_ctx
        )
        key_doc, unused_rope = document_info(key_pos, lengths)
        allowed = (query_doc[:, None] == key_doc[None, :]) & (
            key_pos[None, :] <= query_pos[:, None]
        )
        key_part = block_kv[0].reshape(length_now, key_value_share, HEAD_SIZE)
        value_part = block_kv[1].reshape(length_now, key_value_share, HEAD_SIZE)
        scores = (
            jnp.einsum("qkgd,skd->kgqs", query_groups, key_part, preferred_element_type=jnp.float32)
            * score_scale
        )
        weights = jnp.where(allowed[None, None], jnp.exp(scores), 0.0).astype(jnp.bfloat16)
        numerator = state_now[0] + jnp.einsum(
            "kgqs,skd->qkgd", weights, value_part, preferred_element_type=jnp.float32
        )
        denominator = state_now[1] + jnp.sum(weights, axis=-1, dtype=jnp.float32)
        return (numerator, denominator) + tuple(state_now[2:])

    initial = (
        jnp.zeros((tok_ctx, key_value_share, group_dev, HEAD_SIZE), jnp.float32),
        jnp.zeros((key_value_share, group_dev, tok_ctx), jnp.float32),
    )
    first_state = attend(initial, key_values, my_ctx * tok_ctx)

    def turn(step_no, loop_state):
        moving = from_behind(loop_state[0], "ctx", 1)
        source = (my_ctx - step_no) % count_ctx
        return (moving, attend(loop_state[1], moving, source * tok_ctx))

    final_state = lax.fori_loop(1, count_ctx, turn, (key_values, first_state))[1]
    context = (
        (final_state[0] / jnp.transpose(final_state[1], (2, 0, 1))[..., None])
        .astype(jnp.bfloat16)
        .reshape(tok_ctx, q_dev * HEAD_SIZE)
    )
    own_cols = lax.dynamic_slice_in_dim(key_values, col_offset, column_share, 2)
    every_rows = lax.all_gather(own_cols, "ctx", axis=1, tiled=True)

    def block_start(block_no):
        holder = jnp.where(block_no < count_ctx, block_no, 2 * count_ctx - 1 - block_no)
        return holder * tok_ctx + jnp.where(block_no < count_ctx, 0, half_rows)

    first_part = lax.dynamic_slice_in_dim(every_rows, block_start(2 * my_ctx), half_rows, 1)
    second_part = lax.dynamic_slice_in_dim(every_rows, block_start(2 * my_ctx + 1), half_rows, 1)
    cache = jnp.concatenate([first_part, second_part], axis=1)
    attn_part = jnp.dot(
        context,
        lax.all_gather(o_weight, "ctx", axis=1, tiled=True),
        preferred_element_type=jnp.float32,
    )
    attn_own = lax.psum_scatter(
        attn_part.astype(jnp.bfloat16), "exp", scatter_dimension=0, tiled=True
    ).astype(jnp.float32)
    residual_mid = hidden.astype(jnp.float32) + attn_own
    moe_in = rms_scale(residual_mid, moe_gain).astype(jnp.bfloat16)
    devices = count_ctx * expert_count
    slices = max(1, devices // EXPERTS)
    rows_dev = expert_in.shape[0]
    ffs_dev = expert_out.shape[1]
    capacity = max(4, 2 * tok_dev * TOP // EXPERTS)
    route_ids = routes.reshape(-1)
    route_count = route_ids.shape[0]
    expert_hot = (route_ids[:, None] == jnp.arange(EXPERTS, dtype=jnp.int32)[None, :]).astype(
        jnp.int32
    )
    ranking = jnp.sum(jnp.cumsum(expert_hot, axis=0) * expert_hot, axis=1) - 1
    slot_ids = route_ids * capacity + ranking
    slot_hot = (
        slot_ids[:, None] == jnp.arange(EXPERTS * capacity, dtype=jnp.int32)[None, :]
    ).astype(jnp.bfloat16)
    token_hot = (
        (jnp.arange(route_count, dtype=jnp.int32) // TOP)[:, None]
        == jnp.arange(tok_dev, dtype=jnp.int32)[None, :]
    ).astype(jnp.bfloat16)
    placement_map = jnp.einsum(
        "rs,rt->st", slot_hot, token_hot, preferred_element_type=jnp.float32
    ).astype(jnp.bfloat16)
    outgoing = jnp.dot(placement_map, moe_in, preferred_element_type=jnp.float32).astype(
        jnp.bfloat16
    )
    outgoing = jnp.broadcast_to(
        outgoing.reshape(EXPERTS, 1, capacity, MODEL_WIDTH),
        (EXPERTS, slices, capacity, MODEL_WIDTH),
    )
    outgoing = outgoing.reshape(count_ctx, expert_count, rows_dev * capacity, MODEL_WIDTH)
    arrived = lax.all_to_all(
        lax.all_to_all(outgoing, "ctx", split_axis=0, concat_axis=0, tiled=True),
        "exp",
        split_axis=1,
        concat_axis=1,
        tiled=True,
    )
    arrived = arrived.reshape(count_ctx, expert_count, rows_dev, capacity, MODEL_WIDTH)
    gate_up = jnp.einsum("abrcd,rdf->abrcf", arrived, expert_in, preferred_element_type=jnp.float32)
    activated = (jax.nn.silu(gate_up[..., :ffs_dev]) * gate_up[..., ffs_dev:]).astype(jnp.bfloat16)
    produced = jnp.einsum(
        "abrcf,rfd->abrcd", activated, expert_out, preferred_element_type=jnp.float32
    ).astype(jnp.bfloat16)
    produced = produced.reshape(count_ctx, expert_count, rows_dev * capacity, MODEL_WIDTH)
    returned = lax.all_to_all(
        lax.all_to_all(produced, "ctx", split_axis=0, concat_axis=0, tiled=True),
        "exp",
        split_axis=1,
        concat_axis=1,
        tiled=True,
    )
    slice_sum = jnp.sum(
        returned.reshape(EXPERTS, slices, capacity, MODEL_WIDTH), axis=1, dtype=jnp.float32
    ).reshape(EXPERTS * capacity, MODEL_WIDTH)
    gate_hot = slot_hot.astype(jnp.float32) * gates.reshape(-1)[:, None]
    combiner = jnp.einsum(
        "rs,rt->ts", gate_hot, token_hot.astype(jnp.float32), precision=lax.Precision.HIGHEST
    )
    moe_out = jnp.dot(combiner, slice_sum, precision=lax.Precision.HIGHEST)
    new_hidden = (residual_mid + moe_out).astype(jnp.bfloat16)
    return (new_hidden, cache)


def solution(mesh):
    in_specs = (
        P(("ctx", "exp"), None),
        P(),
        P(("ctx", "exp"), None),
        P(("ctx", "exp"), None),
        P(),
        P("ctx", "exp"),
        P("ctx", None),
        P(),
        P(),
        P("exp", "ctx"),
        P(),
        P(("ctx", "exp"), None, None),
        P(("ctx", "exp"), None, None),
    )
    out_specs = (P(("ctx", "exp"), None), P(None, "ctx", "exp"))
    return jax.shard_map(shards, mesh=mesh, in_specs=in_specs, out_specs=out_specs, check_vma=False)
```

profile of v0, /device:TPU:10, one launch (start us, length us, event | category | flops | bytes accessed | tf_op | source)
XLA Modules:
  0.0 1097.1 jit_solution(15712542725052238022)
XLA Ops:
  8.4 2.0 fusion.42
  18.5 14.6 %all-gather.6.cloned.1.call-done = bf16[256,2048]{1,0:T(8,128)(2,1)} async-done(((bf16[128,2048]{1,0:T(8,128)(2,1)}), bf16[256,2048]{1,0:T(8,128)(2,1)}) %all-gather.6.cloned.1.call-update) | async-done | bytes 1048592 | tf_op jit(solution)/shard_map/all_gather | solution.py:100
  33.1 42.3 %all-gather.8.cloned.1.call-done = bf16[2048,512]{1,0:T(8,128)(2,1)} async-done(((bf16[128,512]{1,0:T(8,128)(2,1)}), bf16[2048,512]{1,0:T(8,128)(2,1)}) %all-gather.8.cloned.1.call-update) | async-done | bytes 2097168 | tf_op jit(solution)/shard_map/all_gather | solution.py:118
  75.4 2.6 fusion.67
  80.9 70.7 %all-gather.10.cloned.1.call-done = bf16[2048,2048]{1,0:T(8,128)(2,1)} async-done(((bf16[128,2048]{1,0:T(8,128)(2,1)}), bf16[2048,2048]{1,0:T(8,128)(2,1)}) %all-gather.10.cloned.1.call-update) | async-done | bytes 8388624 | tf_op jit(solution)/shard_map/all_gather | solution.py:113
  151.7 6.0 convolution_bitcast_fusion.1
  163.1 1.8 convolution_bitcast_fusion
  164.9 1.9 copy.151
  166.9 172.7 %while.22 = (s32[]{:T(128)}, bf16[2,256,256]{1,2,0:T(8,128)(2,1)}, f32[256,2,8,128]{3,0,2,1:T(8,128)S(1)}, f32[2,8,256]{2,1,0:T(8,128)S(1)}, s32[]{:T(128)}, /*i...) while((s32[]{:T(128)}, bf16[2,256,256]{1,2,0:T(8,128)(2,1)}, ...), condition=%wide.region_6.7_spmd.clone.clone, body=%wide.region_4.6_spmd.clone.clone.sunk | while | flops 542874112 | bytes 12001626 | solution.py:172
  168.0 5.0 collective-permute-done
  176.7 5.5 collective-permute-start
  184.8 1.8 bitcast_add_fusion.2
  187.3 5.6 collective-permute-start
  193.7 3.2 collective-permute-done
  200.6 8.7 collective-permute-start
  210.1 2.1 collective-permute-done
  213.4 1.8 bitcast_add_fusion.2
  215.9 7.4 collective-permute-start
  225.9 1.8 bitcast_add_fusion.2
  228.4 9.6 collective-permute-start
  243.4 5.3 collective-permute-start
  254.4 5.0 collective-permute-start
  262.5 1.8 bitcast_add_fusion.2
  265.0 5.0 collective-permute-start
  275.7 5.0 collective-permute-start
  286.3 5.0 collective-permute-start
  297.0 5.0 collective-permute-start
  307.6 5.0 collective-permute-start
  318.3 5.0 collective-permute-start
  328.9 5.0 collective-permute-start
  339.6 1.9 copy.152
  343.3 6.8 convolution_convert_fusion.1
  351.3 44.9 %reduce-scatter.2.cloned.1.call-done = bf16[128,2048]{1,0:T(8,128)(2,1)} async-done(((bf16[256,2048]{1,0:T(8,128)(2,1)}), bf16[128,2048]{1,0:T(8,128)(2,1)}) %reduce-scatter.2.cloned.1.call-update) | async-done | bytes 524304 | tf_op jit(solution)/shard_map/reduce_scatter | solution.py:193
  397.5 9.4 convolution_convert_fusion
  406.9 188.1 %all_to_all.20 = bf16[16,2,64,2048]{3,2,1,0:T(8,128)(2,1)} all-to-all(bf16[16,2,64,2048]{3,2,1,0:T(8,128)(2,1)} %bitcast.119), channel_id=1, replica_groups=mesh['ctx'=16,'exp'=2] {'ctx'}, dimensions={0} | all-to-all | bytes 16777216 | tf_op jit(solution)/shard_map/all_to_all | solution.py:229
  595.0 8.3 copy.158
  603.3 104.1 %all_to_all.21 = bf16[16,2,64,2048]{3,2,0,1:T(8,128)(2,1)} all-to-all(bf16[16,2,64,2048]{3,2,0,1:T(8,128)(2,1)} %copy.158), channel_id=1, replica_groups=mesh['ctx'=16,'exp'=2] {'exp'}, dimensions={1} | all-to-all | bytes 16777216 | tf_op jit(solution)/shard_map/all_to_all | solution.py:228
  707.4 21.7 %fusion.23 = f32[16,2,4,16,1536]{4,3,1,0,2:T(8,128)} fusion(bf16[4,2048,1536]{2,1,0:T(8,128)(2,1)} %param.26, bf16[16,2,4,16,2048]{4,3,2,0,1:T(8,128)(2,1)} %bitcast.122), kind=kOutput, calls=%fused_computation.50 | convolution fusion | flops 12884901888 | bytes 46137344 | tf_op jit(solution)/shard_map/abrcd,rdf->abrcf/dot_general | solution.py:236
  729.1 15.6 %convert_bitcast_fusion = bf16[16,2,4,16,2048]{4,3,1,0,2:T(8,128)(2,1)} fusion(bf16[4,768,2048]{2,1,0:T(8,128)(2,1)} %param.27, f32[16,2,4,16,1536]{4,3,1,0,2:T(8,128)} %fusion.23), kind=kOutput, calls=%fused_computation.42 | convolution fusion | flops 6456082432 | bytes 33554432 | tf_op jit(solution)/shard_map/abrcf,rfd->abrcd/dot_general | solution.py:238
  744.7 8.3 copy.161
  752.9 5.8 all-to-all-start.2
  759.4 206.9 %all-to-all-done.2 = bf16[16,2,64,2048]{3,2,1,0:T(8,128)(2,1)} async-done(((bf16[16,2,64,2048]{3,2,1,0:T(8,128)(2,1)}), bf16[16,2,64,2048]{3,2,1,0:T(8,128)(2,1)}, u32[]{:S(2)}, u32[]{:S(2)}) %all-to-all-start.2) | async-done | bytes 8388640 | tf_op jit(solution)/shard_map/all_to_all | solution.py:243
  966.3 8.3 copy.162
  974.6 7.1 all-to-all-start.3
  981.9 4.3 fusion.18
  987.9 86.8 %all-to-all-done.3 = bf16[16,2,64,2048]{3,2,0,1:T(8,128)(2,1)} async-done(((bf16[16,2,64,2048]{3,2,0,1:T(8,128)(2,1)}), bf16[16,2,64,2048]{3,2,0,1:T(8,128)(2,1)}, u32[]{:S(2)}, u32[]{:S(2)}) %all-to-all-start.3) | async-done | bytes 8388640 | tf_op jit(solution)/shard_map/all_to_all | solution.py:242
  1074.7 8.3 copy.163
  1083.0 6.8 fusion.38
  (222 shorter events, 95.5 us)
Async XLA Ops:
  7.2 26.0 %all-gather.6.cloned.1.call-start = ((), (), s32[]{:S(2)}) async-start(), calls=%async_computation.5 | async-start | bytes 1572864 | tf_op jit(solution)/shard_map/all_gather | solution.py:100
  10.5 64.9 %all-gather.8.cloned.1.call-start = ((), (), s32[]{:S(2)}) async-start(), calls=%async_computation.6 | async-start | bytes 2228224 | tf_op jit(solution)/shard_map/all_gather | solution.py:118
  10.6 68.3 %copy-start.10 = (f32[128]{0:T(128)S(1)}, f32[128]{0:T(128)}, u32[]{:S(2)}) copy-start(f32[128]{0:T(128)} %param.23) | copy-start | bytes 1540
  12.2 139.5 %all-gather.10.cloned.1.call-start = ((), (), s32[]{:S(2)}) async-start(), calls=%async_computation.7 | async-start | bytes 8912896 | tf_op jit(solution)/shard_map/all_gather | solution.py:113
  12.9 330.3 %all-gather.12.cloned.1.call-start = ((), (), s32[]{:S(2)}) async-start(), calls=%async_computation.8 | async-start | bytes 8912896 | tf_op jit(solution)/shard_map/all_gather | solution.py:190
  13.5 382.8 %reduce-scatter.2.cloned.1.call-start = ((), (), s32[]{:S(2)}) async-start(), calls=%async_computation.9 | async-start | bytes 1572864 | tf_op jit(solution)/shard_map/reduce_scatter | solution.py:193
  79.3 0.6 copy-start.3
  80.1 77.7 %copy-start.2 = (bf16[2,256,256]{2,1,0:T(8,128)(2,1)}, bf16[2,256,256]{2,1,0:T(8,128)(2,1)S(1)}, u32[]{:S(2)}) copy-start(bf16[2,256,256]{2,1,0:T(8,128)(2,1)S(1)} %pad_maximum_fusion.1) | copy-start | bytes 786436
  157.7 1.2 copy-start.11
  160.7 1.2 copy-start.4
  160.8 1.2 copy-start.5
  164.9 1.9 copy-start.6
  166.9 6.1 collective-permute-start
  176.7 6.9 collective-permute-start
  187.3 9.6 collective-permute-start
  200.6 11.6 %collective-permute-start = (bf16[2,256,256]{1,2,0:T(8,128)(2,1)}, bf16[2,256,256]{1,2,0:T(8,128)(2,1)S(1)}, u32[]{:S(2)}, u32[]{:S(2)}) collective-permute-start(bf16[2,256,256]{1,2,0:T(8,128)(2,1)} %get-tuple-element.542), channel_id=1, source_target_pairs={{30,0},{0,2},{2,4},{4,6},{6,8},{8,10},{10,12},{12,14},{14,16},{16,... | collective-permute-start | bytes 786440 | tf_op jit(solution)/shard_map/while/body/eval_jaxpr/ppermute | solution.py:21
  215.9 8.8 collective-permute-start
  228.4 11.3 %collective-permute-start = (bf16[2,256,256]{1,2,0:T(8,128)(2,1)}, bf16[2,256,256]{1,2,0:T(8,128)(2,1)S(1)}, u32[]{:S(2)}, u32[]{:S(2)}) collective-permute-start(bf16[2,256,256]{1,2,0:T(8,128)(2,1)} %get-tuple-element.542), channel_id=1, source_target_pairs={{30,0},{0,2},{2,4},{4,6},{6,8},{8,10},{10,12},{12,14},{14,16},{16,... | collective-permute-start | bytes 786440 | tf_op jit(solution)/shard_map/while/body/eval_jaxpr/ppermute | solution.py:21
  243.4 7.2 collective-permute-start
  254.4 6.9 collective-permute-start
  265.0 6.9 collective-permute-start
  275.7 6.9 collective-permute-start
  286.3 6.9 collective-permute-start
  297.0 6.9 collective-permute-start
  307.6 6.9 collective-permute-start
  318.3 6.9 collective-permute-start
  328.9 6.9 collective-permute-start
  343.3 6.9 copy-start.8
  350.1 46.2 %copy-start = (bf16[128,2048]{1,0:T(8,128)(2,1)S(1)}, bf16[128,2048]{1,0:T(8,128)(2,1)}, u32[]{:S(2)}) copy-start(bf16[128,2048]{1,0:T(8,128)(2,1)} %param.15) | copy-start | bytes 1572868
  350.1 47.5 %copy-start.7 = (f32[2048]{0:T(1024)S(1)}, f32[2048]{0:T(1024)}, u32[]{:S(2)}) copy-start(f32[2048]{0:T(1024)} %param.25) | copy-start | bytes 24580
  752.9 213.4 %all-to-all-start.2 = ((bf16[16,2,64,2048]{3,2,1,0:T(8,128)(2,1)}), bf16[16,2,64,2048]{3,2,1,0:T(8,128)(2,1)}, u32[]{:S(2)}, u32[]{:S(2)}) async-start(bf16[16,2,64,2048]{3,2,1,0:T(8,128)(2,1)} %bitcast.118), calls=%async_computation.3 | async-start | bytes 16777216 | tf_op jit(solution)/shard_map/all_to_all | solution.py:243
  758.8 227.4 %all-gather.14.cloned.1.call-start = ((), (), s32[]{:S(2)}) async-start(), calls=%async_computation.10 | async-start | bytes 4456448 | tf_op jit(solution)/shard_map/all_gather | solution.py:179
  974.6 7.1 copy-start.9
  974.6 100.2 %all-to-all-start.3 = ((bf16[16,2,64,2048]{3,2,0,1:T(8,128)(2,1)}), bf16[16,2,64,2048]{3,2,0,1:T(8,128)(2,1)}, u32[]{:S(2)}, u32[]{:S(2)}) async-start(bf16[16,2,64,2048]{3,2,0,1:T(8,128)(2,1)} %copy.162), calls=%async_computation.4 | async-start | bytes 16777216 | tf_op jit(solution)/shard_map/all_to_all | solution.py:242
  987.9 95.1 %copy-start.1 = (bf16[128,2048]{1,0:T(8,128)(2,1)S(1)}, bf16[128,2048]{1,0:T(8,128)(2,1)}, u32[]{:S(2)}) copy-start(bf16[128,2048]{1,0:T(8,128)(2,1)} %reduce-scatter.2.cloned.1.call-done) | copy-start | bytes 1572868
Sparse Core Ops, SparseCore 0:
  10.6 22.4 all-gather.5
  35.8 39.5 all-gather.7
  77.6 74.0 all-gather.9
  153.7 85.9 all-gather.11
  350.2 45.9 reduce-scatter.1
  762.3 158.9 all-gather.13
where the time goes:
time: 1100 us
  waiting for transfers between devices  491 us (45%)
  blocking collectives  292 us (27%)
  matrix products  121 us (11%)
  starting transfers between devices  95.5 us (9%)
  local copies, waits for them, and re-layouts  54.7 us (5%)
  other arithmetic  26.3 us (2%)
  between operations  16.1 us (1%)
    all_to_all x1, waiting for transfers between devices, shards(): lax.all_to_all(produced, 'ctx', split_axis=0, concat_axis=0, tiled=True)  207 us
    all_to_all x1, blocking collectives, shards(): lax.all_to_all(outgoing, 'ctx', split_axis=0, concat_axis=0, tiled=True)  188 us
    all_to_all x1, blocking collectives, shards(): lax.all_to_all(lax.all_to_all(outgoing, 'ctx', split_axis=0, concat_axis=...  104 us
    all_to_all x1, waiting for transfers between devices, shards(): lax.all_to_all(lax.all_to_all(produced, 'ctx', split_axis=0, concat_axis=...  86.8 us
    ppermute x15, starting transfers between devices, from_behind(): return lax.ppermute(block, axis, route)  82.1 us
    all_gather x1, waiting for transfers between devices, shards(): lax.all_gather(q_weight, 'ctx', axis=0, tiled=True)  70.7 us
    reduce_scatter x1, waiting for transfers between devices, shards(): lax.psum_scatter(attn_part.astype(jnp.bfloat16), 'exp', scatter_dimension...  44.9 us
    all_gather x1, waiting for transfers between devices, shards(): lax.all_gather(kv_local, 'ctx', axis=0, tiled=True)  42.3 us
  transfers between devices with their start and end apart: 23, of which 21 were waited for; matrix products, arithmetic and copies ran while one was open for 10% of the time, Pallas kernels for 0%

commit v1 on v0

v1 whole, which is shorter than its diff:
```python
import functools
import jax
import jax.numpy as jnp
from jax import lax
from jax.experimental import pallas as pl
from jax.experimental.pallas import tpu as pltpu
from jax.sharding import PartitionSpec as P

MODEL_WIDTH = 2048
QUERY_HEADS = 32
KEY_VALUE_HEADS = 4
HEAD_SIZE = 128
EXPERTS = 128
TOP = 8


epsilon = 1e-06
rope_base = 1000000.0


def rms_scale(values, gain):
    mean_square = jnp.mean(values * values, axis=-1, keepdims=True)
    return values * lax.rsqrt(mean_square + epsilon) * gain


def mirrored_position(row_ids, count_ctx, tok_ctx):
    half_rows = tok_ctx // 2
    holder = row_ids // tok_ctx
    within = row_ids % tok_ctx
    block_no = jnp.where(within < half_rows, holder, 2 * count_ctx - 1 - holder)
    return block_no * half_rows + within % half_rows


def document_info(token_positions, lengths):
    first_end = lengths[0]
    second_end = lengths[0] + lengths[1]
    document = (token_positions >= first_end).astype(jnp.int32) + (
        token_positions >= second_end
    ).astype(jnp.int32)
    doc_start = jnp.where(document == 0, 0, jnp.where(document == 1, first_end, second_end))
    return (document, token_positions - doc_start)


def rotate(values, rope_pos):
    head_width = values.shape[-1]
    freq_ids = jnp.arange(head_width // 2, dtype=jnp.float32)
    inverse = rope_base ** (-2.0 * freq_ids / head_width)
    angles = rope_pos.astype(jnp.float32)[:, None] * inverse[None, :]
    cosine = jnp.cos(angles)[:, None, :]
    sine_part = jnp.sin(angles)[:, None, :]
    first_half = values[..., : head_width // 2]
    second_half = values[..., head_width // 2 :]
    return jnp.concatenate(
        [
            first_half * cosine - second_half * sine_part,
            second_half * cosine + first_half * sine_part,
        ],
        axis=-1,
    )


MESH = pl.DeviceIdType.MESH
CHUNKS = 4
KEY_TILE = 256


def attention_kernel(count_ctx, half_rows, group, len_ref, q_ref, k_ref, v_ref, o_ref, q_all, total):
    my_ctx = lax.axis_index("ctx")
    first_end = len_ref[0]
    second_end = len_ref[0] + len_ref[1]
    score_scale = HEAD_SIZE ** (-0.5)
    ones = jnp.ones((KEY_TILE, HEAD_SIZE), jnp.bfloat16)

    def doc_of(pos):
        return (pos >= first_end).astype(jnp.int32) + (pos >= second_end).astype(jnp.int32)

    for half in range(2):
        block_no = my_ctx if half == 0 else 2 * count_ctx - 1 - my_ctx
        start = block_no * half_rows
        rows = pl.ds(half * half_rows, half_rows)
        for head in range(group):
            q_all[pl.ds(head * half_rows, half_rows), :] = q_ref[
                rows, pl.ds(head * HEAD_SIZE, HEAD_SIZE)
            ]
        total[...] = jnp.zeros_like(total)
        doc_start = jnp.where(
            start >= second_end, second_end, jnp.where(start >= first_end, first_end, 0)
        )
        query_pos = start + lax.broadcasted_iota(jnp.int32, (half_rows, KEY_TILE), 0)
        query_doc = doc_of(query_pos)

        def tile(index, carry):
            keys = k_ref[pl.ds(pl.multiple_of(index * KEY_TILE, KEY_TILE), KEY_TILE), :]
            values = v_ref[pl.ds(pl.multiple_of(index * KEY_TILE, KEY_TILE), KEY_TILE), :]
            key_pos = index * KEY_TILE + lax.broadcasted_iota(
                jnp.int32, (half_rows, KEY_TILE), 1
            )
            allowed = (doc_of(key_pos) == query_doc) & (key_pos <= query_pos)
            scores = lax.dot_general(
                q_all[...], keys, (((1,), (1,)), ((), ())), preferred_element_type=jnp.float32
            )
            scores = (scores * score_scale).reshape(group, half_rows, KEY_TILE)
            weights = jnp.where(allowed[None], jnp.exp(scores), 0.0).astype(jnp.bfloat16)
            total[...] += jnp.dot(
                weights.reshape(group * half_rows, KEY_TILE),
                jnp.concatenate([values, ones], axis=1),
                preferred_element_type=jnp.float32,
            )
            return carry

        lax.fori_loop(
            doc_start // KEY_TILE, (start + half_rows - 1) // KEY_TILE + 1, tile, 0
        )
        result = (total[:, :HEAD_SIZE] / total[:, HEAD_SIZE:]).astype(jnp.bfloat16)
        for head in range(group):
            o_ref[rows, pl.ds(head * HEAD_SIZE, HEAD_SIZE)] = result[
                head * half_rows : (head + 1) * half_rows
            ]


def attention(lengths, queries, keys, values, count_ctx, half_rows, share, group):
    length = keys.shape[0]
    width = group * HEAD_SIZE
    return pl.pallas_call(
        functools.partial(attention_kernel, count_ctx, half_rows, group),
        grid=(share,),
        in_specs=[
            pl.BlockSpec(memory_space=pltpu.SMEM),
            pl.BlockSpec((2 * half_rows, width), lambda i: (0, i)),
            pl.BlockSpec((length, HEAD_SIZE), lambda i: (0, i)),
            pl.BlockSpec((length, HEAD_SIZE), lambda i: (0, i)),
        ],
        out_specs=pl.BlockSpec((2 * half_rows, width), lambda i: (0, i)),
        out_shape=jax.ShapeDtypeStruct((2 * half_rows, share * width), jnp.bfloat16),
        scratch_shapes=[
            pltpu.VMEM((group * half_rows, HEAD_SIZE), jnp.bfloat16),
            pltpu.VMEM((group * half_rows, 2 * HEAD_SIZE), jnp.float32),
        ],
        compiler_params=pltpu.CompilerParams(vmem_limit_bytes=40 * 1024 * 1024),
        name="attention",
    )(lengths, queries, keys, values)


def reduce_kernel(
    Z, E, p_ref, o_ref, held, from_core, from_e, from_x, from_z, load_sem, send_sem, recv_sem
):
    ctx = lax.axis_index("ctx")
    e = lax.axis_index("exp")
    core = lax.rem(ctx, 2)
    x = lax.rem(ctx // 2, 2)
    z = ctx // 4
    width = held.shape[-1]
    sibling = (ctx + 1 - 2 * core, e)
    x_peer = (ctx + 2 - 4 * x, e)
    e_peer = [(ctx, lax.rem(e + d, E)) for d in range(1, E)]
    z_peer = [(lax.rem(z + d, Z) * 4 + lax.rem(ctx, 4), e) for d in range(1, Z)]
    z_next = [lax.rem(z + d, Z) for d in range(1, Z)]
    e_next = [lax.rem(e + d, E) for d in range(1, E)]

    barrier = pltpu.get_barrier_semaphore()
    peers = [sibling, x_peer] + e_peer + z_peer
    for peer in peers:
        pl.semaphore_signal(barrier, inc=1, device_id=peer, device_id_type=MESH)
    pl.semaphore_wait(barrier, len(peers))

    def remote(src, dst, k, slot, peer):
        copy = pltpu.make_async_remote_copy(
            src_ref=src,
            dst_ref=dst,
            send_sem=send_sem.at[k, slot],
            recv_sem=recv_sem.at[k, slot],
            device_id=peer,
            device_id_type=MESH,
        )
        copy.start()
        return copy

    def add(target, sources):
        value = target[...].astype(jnp.float32)
        for source in sources:
            value = value + source[...].astype(jnp.float32)
        target[...] = value.astype(jnp.bfloat16)

    first, local = [], []
    for k in range(CHUNKS):
        columns = pl.ds(k * width, width)
        first.append(
            remote(p_ref.at[:, :, 1 - core, :, :, columns], from_core.at[k], k, 0, sibling)
        )
        copy = pltpu.make_async_copy(
            p_ref.at[:, :, core, :, :, columns], held.at[k], load_sem.at[k]
        )
        copy.start()
        local.append(copy)

    def send_e(k, x_first):
        out = []
        for d in range(1, E):
            if x_first:
                src = held.at[k, :, x, e_next[d - 1]]
                dst = from_e.at[k, d - 1, :, 0]
            else:
                src = held.at[k, :, :, e_next[d - 1]]
                dst = from_e.at[k, d - 1]
            out.append(remote(src, dst, k, d, e_peer[d - 1]))
        return out

    def send_x(k, x_first):
        if x_first:
            return [remote(held.at[k, :, 1 - x], from_x.at[k], k, E, x_peer)]
        return [remote(held.at[k, :, 1 - x, e], from_x.at[k, :, 0], k, E, x_peer)]

    def add_e(k, x_first):
        @pl.loop(0, Z)
        def _(i):
            if x_first:
                add(held.at[k, i, x, e], [from_e.at[k, d, i, 0] for d in range(E - 1)])
            else:
                for j in range(2):
                    add(held.at[k, i, j, e], [from_e.at[k, d, i, j] for d in range(E - 1)])

    def add_x(k, x_first):
        @pl.loop(0, Z)
        def _(i):
            if x_first:

                @pl.loop(0, E)
                def _(j):
                    add(held.at[k, i, x, j], [from_x.at[k, i, j]])

            else:
                add(held.at[k, i, x, e], [from_x.at[k, i, 0]])

    flying = []
    sent = []
    for k in range(CHUNKS):
        local[k].wait()
        first[k].wait_recv()

        @pl.loop(0, Z)
        def _(i):
            @pl.loop(0, E)
            def _(j):
                for m in range(2):
                    add(held.at[k, i, m, j], [from_core.at[k, i, m, j]])

        flying.append(send_x(k, True) if k % 2 else send_e(k, False))
    sent += first
    for k in range(CHUNKS):
        for copy in flying[k]:
            copy.wait_recv()
        sent += flying[k]
        if k % 2:
            add_x(k, True)
            flying[k] = send_e(k, True)
        else:
            add_e(k, False)
            flying[k] = send_x(k, False)
    for k in range(CHUNKS):
        for copy in flying[k]:
            copy.wait_recv()
        sent += flying[k]
        if k % 2:
            add_e(k, True)
        else:
            add_x(k, False)
        flying[k] = [
            remote(held.at[k, z_next[d - 1], x, e], from_z.at[k, d - 1], k, E + d, z_peer[d - 1])
            for d in range(1, Z)
        ]
    for k in range(CHUNKS):
        for copy in flying[k]:
            copy.wait_recv()
        sent += flying[k]
        value = held[k, z, x, e].astype(jnp.float32)
        for d in range(Z - 1):
            value = value + from_z[k, d].astype(jnp.float32)
        o_ref[:, k * width : (k + 1) * width] = value
    for copy in sent:
        copy.wait_send()


def reduce_over_devices(partial, count_ctx, expert_count, tok_dev):
    Z = count_ctx // 4
    E = expert_count
    width = MODEL_WIDTH // CHUNKS
    slots = E + Z
    return pl.pallas_call(
        functools.partial(reduce_kernel, Z, E),
        in_specs=[pl.BlockSpec(memory_space=pl.ANY)],
        out_specs=pl.BlockSpec(memory_space=pltpu.VMEM),
        out_shape=jax.ShapeDtypeStruct((tok_dev, MODEL_WIDTH), jnp.float32),
        scratch_shapes=[
            pltpu.VMEM((CHUNKS, Z, 2, E, tok_dev, width), jnp.bfloat16),
            pltpu.VMEM((CHUNKS, Z, 2, E, tok_dev, width), jnp.bfloat16),
            pltpu.VMEM((CHUNKS, E - 1, Z, 2, tok_dev, width), jnp.bfloat16),
            pltpu.VMEM((CHUNKS, Z, E, tok_dev, width), jnp.bfloat16),
            pltpu.VMEM((CHUNKS, Z - 1, tok_dev, width), jnp.bfloat16),
            pltpu.SemaphoreType.DMA((CHUNKS,)),
            pltpu.SemaphoreType.DMA((CHUNKS, slots)),
            pltpu.SemaphoreType.DMA((CHUNKS, slots)),
        ],
        compiler_params=pltpu.CompilerParams(
            collective_id=0, has_side_effects=True, vmem_limit_bytes=VMEM_LIMIT
        ),
        name="reduce_over_devices",
    )(partial.reshape(Z, 2, 2, E, tok_dev, MODEL_WIDTH))


VMEM_LIMIT = 60 * 1024 * 1024


def shards(
    hidden,
    lengths,
    routes,
    gates,
    attn_gain,
    q_weight,
    key_value_weight,
    q_gain,
    k_gain,
    o_weight,
    moe_gain,
    expert_in,
    expert_out,
):
    count_ctx = lax.axis_size("ctx")
    expert_count = lax.axis_size("exp")
    my_ctx = lax.axis_index("ctx")
    my_exp = lax.axis_index("exp")
    tok_dev = hidden.shape[0]
    tok_ctx = tok_dev * expert_count
    half_rows = tok_ctx // 2
    head_groups = QUERY_HEADS // KEY_VALUE_HEADS
    q_dev = QUERY_HEADS // expert_count
    key_value_share = max(1, KEY_VALUE_HEADS // expert_count)
    group_dev = q_dev // key_value_share
    column_share = KEY_VALUE_HEADS * HEAD_SIZE // expert_count
    key_value_leading = my_exp * q_dev // head_groups
    col_offset = my_exp * column_share - key_value_leading * HEAD_SIZE
    query_pos = mirrored_position(
        my_ctx * tok_ctx + jnp.arange(tok_ctx, dtype=jnp.int32), count_ctx, tok_ctx
    )
    query_doc, query_rope = document_info(query_pos, lengths)
    normed_own = rms_scale(hidden.astype(jnp.float32), attn_gain).astype(jnp.bfloat16)
    normed = lax.all_gather(normed_own, "exp", axis=0, tiled=True)
    key_cols = lax.dynamic_slice_in_dim(
        key_value_weight, key_value_leading * HEAD_SIZE, key_value_share * HEAD_SIZE, 1
    )
    value_column_block = lax.dynamic_slice_in_dim(
        key_value_weight,
        KEY_VALUE_HEADS * HEAD_SIZE + key_value_leading * HEAD_SIZE,
        key_value_share * HEAD_SIZE,
        1,
    )
    kv_local = jnp.concatenate([key_cols, value_column_block], axis=1)
    q_raw = jnp.dot(
        normed,
        lax.all_gather(q_weight, "ctx", axis=0, tiled=True),
        preferred_element_type=jnp.float32,
    )
    key_value_plain = jnp.dot(
        normed,
        lax.all_gather(kv_local, "ctx", axis=0, tiled=True),
        preferred_element_type=jnp.float32,
    )
    queries = rotate(
        rms_scale(q_raw.reshape(tok_ctx, q_dev, HEAD_SIZE), q_gain), query_rope
    ).astype(jnp.bfloat16)
    key_row_block = rotate(
        rms_scale(
            key_value_plain[:, : key_value_share * HEAD_SIZE].reshape(
                tok_ctx, key_value_share, HEAD_SIZE
            ),
            k_gain,
        ),
        query_rope,
    ).astype(jnp.bfloat16)
    value_row_block = key_value_plain[:, key_value_share * HEAD_SIZE :].astype(jnp.bfloat16)
    key_values = jnp.stack(
        [key_row_block.reshape(tok_ctx, key_value_share * HEAD_SIZE), value_row_block]
    )
    gathered = lax.all_gather(key_values, "ctx", axis=0)
    ordered = jnp.concatenate(
        [
            jnp.moveaxis(gathered[:, :, :half_rows], 0, 1),
            jnp.moveaxis(gathered[::-1, :, half_rows:], 0, 1),
        ],
        axis=1,
    ).reshape(2, count_ctx * tok_ctx, key_value_share * HEAD_SIZE)
    cache = lax.dynamic_slice(
        ordered, (0, my_ctx * tok_ctx, col_offset), (2, tok_ctx, column_share)
    )
    context = attention(
        lengths,
        queries.reshape(tok_ctx, q_dev * HEAD_SIZE),
        ordered[0],
        ordered[1],
        count_ctx,
        half_rows,
        key_value_share,
        group_dev,
    )
    o_rows = lax.all_gather(o_weight.T, "ctx", axis=0, tiled=True)
    attn_part = lax.dot_general(
        context, o_rows, (((1,), (1,)), ((), ())), preferred_element_type=jnp.float32
    )
    attn_parts = attn_part.reshape(expert_count, tok_dev, MODEL_WIDTH)
    attn_own = lax.dynamic_index_in_dim(attn_parts, my_exp, 0, keepdims=False)
    for shift in range(1, expert_count):
        outgoing = lax.dynamic_index_in_dim(
            attn_parts, (my_exp + shift) % expert_count, 0, keepdims=False
        ).astype(jnp.bfloat16)
        route = [(i, (i + shift) % expert_count) for i in range(expert_count)]
        attn_own = attn_own + lax.ppermute(outgoing, "exp", route).astype(jnp.float32)
    residual_mid = hidden.astype(jnp.float32) + attn_own
    moe_in = rms_scale(residual_mid, moe_gain).astype(jnp.bfloat16)
    devices = count_ctx * expert_count
    slices = max(1, devices // EXPERTS)
    rows_dev = expert_in.shape[0]
    ffs_dev = expert_out.shape[1]
    capacity = max(4, 2 * tok_dev * TOP // EXPERTS)
    tokens = lax.all_gather(moe_in, ("ctx", "exp"), axis=0)
    table = lax.all_gather(
        jnp.concatenate([routes.astype(jnp.float32), gates], axis=1), ("ctx", "exp"), axis=0
    )
    my_device = my_ctx * expert_count + my_exp
    my_experts = (my_device * rows_dev + jnp.arange(rows_dev, dtype=jnp.int32)) // slices
    chosen = (
        table[:, None, :, :TOP].astype(jnp.int32) == my_experts[None, :, None, None]
    )
    hit = jnp.any(chosen, axis=3)
    token_gate = jnp.sum(jnp.where(chosen, table[:, None, :, TOP:], 0.0), axis=3)
    before = jnp.triu(jnp.ones((tok_dev, tok_dev), jnp.bfloat16), 1)
    ranking = jnp.einsum(
        "ait,tu->aiu", hit.astype(jnp.bfloat16), before, preferred_element_type=jnp.float32
    ).astype(jnp.int32)
    placed = hit[:, :, None, :] & (
        ranking[:, :, None, :] == jnp.arange(capacity, dtype=jnp.int32)[None, None, :, None]
    )
    slot_gate = jnp.sum(jnp.where(placed, token_gate[:, :, None, :], 0.0), axis=3)
    placement = placed.astype(jnp.bfloat16).reshape(devices, rows_dev * capacity, tok_dev)
    arrived = (
        jnp.einsum("ast,atd->asd", placement, tokens, preferred_element_type=jnp.float32)
        .astype(jnp.bfloat16)
        .reshape(devices, rows_dev, capacity, MODEL_WIDTH)
    )
    gate_up = jnp.einsum("arcd,rdf->arcf", arrived, expert_in, preferred_element_type=jnp.float32)
    activated = (
        jax.nn.silu(gate_up[..., :ffs_dev]) * gate_up[..., ffs_dev:] * slot_gate[..., None]
    ).astype(jnp.bfloat16)
    produced = jnp.einsum(
        "arcf,rfd->arcd", activated, expert_out, preferred_element_type=jnp.float32
    ).astype(jnp.bfloat16)
    partial = jnp.einsum(
        "ast,asd->atd",
        placement,
        produced.reshape(devices, rows_dev * capacity, MODEL_WIDTH),
        preferred_element_type=jnp.float32,
    ).astype(jnp.bfloat16)
    moe_out = reduce_over_devices(partial, count_ctx, expert_count, tok_dev)
    new_hidden = (residual_mid + moe_out).astype(jnp.bfloat16)
    return (new_hidden, cache)


def solution(mesh):
    in_specs = (
        P(("ctx", "exp"), None),
        P(),
        P(("ctx", "exp"), None),
        P(("ctx", "exp"), None),
        P(),
        P("ctx", "exp"),
        P("ctx", None),
        P(),
        P(),
        P("exp", "ctx"),
        P(),
        P(("ctx", "exp"), None, None),
        P(("ctx", "exp"), None, None),
    )
    out_specs = (P(("ctx", "exp"), None), P(None, "ctx", "exp"))
    return jax.shard_map(shards, mesh=mesh, in_specs=in_specs, out_specs=out_specs, check_vma=False)
```

time: 1100 us -> 621 us (0.56)
  blocking collectives: 292 us -> 54.2 us
  waiting for transfers between devices: 491 us -> 299 us
  Pallas kernels: 0 us -> 129 us
  starting transfers between devices: 95.5 us -> 2.04 us
  matrix products: 121 us -> 77.1 us
  local copies, waits for them, and re-layouts: 54.7 us -> 21.6 us
    all_to_all x2 -> x0, waiting for transfers between devices: 294 us -> none  [the longest x1 207 us: shards(): lax.all_to_all(produced, 'ctx', split_axis=0, concat_axis=0, tiled=True)]
    all_to_all x2 -> x0, blocking collectives: 292 us -> none  [the longest x1 188 us: shards(): lax.all_to_all(outgoing, 'ctx', split_axis=0, concat_axis=0, tiled=True)]
    all_gather x2 -> x3, waiting for transfers between devices: 0.04 us -> 157 us  [the longest x1 56.9 us: shards(): tokens = lax.all_gather(moe_in, ('ctx', 'exp'), axis=0)]
    pallas_call x0 -> x2, Pallas kernels: none -> 129 us  [the longest x1 116 us: reduce_over_devices(): pl.pallas_call(functools.partial(reduce_kernel, Z, E), in_specs=[pl.Block...]
    ppermute x15 -> x1, starting transfers between devices: 82.1 us -> 1.62 us  [shards(): lax.ppermute(outgoing, 'exp', route).astype(jnp.float32)]
    all_gather x0 -> x1, blocking collectives: none -> 54.2 us  [shards(): lax.all_gather(jnp.concatenate([routes.astype(jnp.float32), gates], axis=...]
    reduce_scatter x1 -> x0, waiting for transfers between devices: 44.9 us -> none  [shards(): lax.psum_scatter(attn_part.astype(jnp.bfloat16), 'exp', scatter_dimension...]
    dot_general x38 -> x6, matrix products: 112 us -> 68.8 us  [the longest x1 21.8 us: shards(): jnp.einsum('arcd,rdf->arcf', arrived, expert_in, preferred_element_type=j...]
  transfers between devices with their start and end apart: 23 -> 7, of which waited for: 21 -> 7; matrix products, arithmetic and copies ran while one was open for 10% -> 4% of each run, Pallas kernels for 0% -> 2%
where the time goes in v1:
time: 621 us; the launch traced here: 620 us
  waiting for transfers between devices  299 us (48%)
  Pallas kernels  129 us (21%)
  matrix products  77.1 us (12%)
  blocking collectives  54.2 us (9%)
  local copies, waits for them, and re-layouts  21.6 us (3%)
  other arithmetic  21.1 us (3%)
  between operations  15.8 us (3%)
    pallas_call x1, Pallas kernels, reduce_over_devices(): pl.pallas_call(functools.partial(reduce_kernel, Z, E), in_specs=[pl.Block...  116 us
    all_gather x1, waiting for transfers between devices, shards(): lax.all_gather(q_weight, 'ctx', axis=0, tiled=True)  67.9 us
    all_gather x1, waiting for transfers between devices, shards(): tokens = lax.all_gather(moe_in, ('ctx', 'exp'), axis=0)  56.9 us
    all_gather x1, blocking collectives, shards(): lax.all_gather(jnp.concatenate([routes.astype(jnp.float32), gates], axis=...  54.2 us
    all_gather x1, waiting for transfers between devices, shards(): o_rows = lax.all_gather(o_weight.T, 'ctx', axis=0, tiled=True)  51.4 us
    all_gather x1, waiting for transfers between devices, shards(): gathered = lax.all_gather(key_values, 'ctx', axis=0)  49.2 us
    all_gather x1, waiting for transfers between devices, shards(): lax.all_gather(kv_local, 'ctx', axis=0, tiled=True)  42.3 us
    dot_general x1, matrix products, shards(): jnp.einsum('arcd,rdf->arcf', arrived, expert_in, preferred_element_type=j...  21.8 us
  transfers between devices with their start and end apart: 7, of which 7 were waited for; matrix products, arithmetic and copies ran while one was open for 4% of the time, Pallas kernels for 2%

profile of v1, /device:TPU:10, one launch (start us, length us, event | category | flops | bytes accessed | tf_op | source)
XLA Modules:
  0.0 619.5 jit_solution(1685168138591029483)
XLA Ops:
  7.2 1.2 fusion.19
  8.5 2.0 fusion.21
  10.6 0.9 constant_dynamic-slice_fusion.2
  11.5 0.7 pad_maximum_fusion.3
  12.2 1.4 fusion.44
  14.9 0.6 fusion.37
  15.5 0.5 multiply_cosine_fusion
  16.0 17.1 %all-gather.10.cloned.1.call-done = bf16[256,2048]{1,0:T(8,128)(2,1)} async-done(((bf16[128,2048]{1,0:T(8,128)(2,1)}), bf16[256,2048]{1,0:T(8,128)(2,1)}) %all-gather.10.cloned.1.call-update) | async-done | bytes 1048592 | tf_op jit(solution)/shard_map/all_gather | solution.py:347
  33.1 42.3 %all-gather.14.cloned.1.call-done = bf16[2048,512]{1,0:T(8,128)(2,1)} async-done(((bf16[128,512]{1,0:T(8,128)(2,1)}), bf16[2048,512]{1,0:T(8,128)(2,1)}) %all-gather.14.cloned.1.call-update) | async-done | bytes 2097168 | tf_op jit(solution)/shard_map/all_gather | solution.py:365
  75.4 2.6 fusion.45
  79.0 0.5 subtract_convert_fusion.1
  79.9 0.7 pad_maximum_fusion.2
  80.7 0.5 all-gather.12.cloned.1.call-update
  81.3 0.5 all-gather.16.cloned.1.call-update
  82.1 49.2 %all-gather.18.cloned.1.call-done = bf16[32,256,256]{2,1,0:T(8,128)(2,1)} async-done(((bf16[2,256,256]{2,1,0:T(8,128)(2,1)}), bf16[32,256,256]{2,1,0:T(8,128)(2,1)}) %all-gather.18.cloned.1.call-update) | async-done | bytes 4194320 | tf_op jit(solution)/shard_map/all_gather | solution.py:384
  131.3 2.7 fusion.42
  134.2 0.5 copy_bitcast_fusion
  134.7 1.3 copy-done.3
  136.0 0.7 copy-done.5
  136.7 1.5 fusion.18
  138.2 67.9 %all-gather.12.cloned.1.call-done = bf16[2048,2048]{1,0:T(8,128)(2,1)} async-done(((bf16[128,2048]{1,0:T(8,128)(2,1)}), bf16[2048,2048]{1,0:T(8,128)(2,1)}) %all-gather.12.cloned.1.call-update) | async-done | bytes 8388624 | tf_op jit(solution)/shard_map/all_gather | solution.py:360
  206.1 5.7 convolution_bitcast_fusion
  212.2 1.4 copy-done.2
  213.6 0.6 multiply_reduce_fusion
  214.4 2.0 multiply_multiply_fusion
  216.5 0.8 subtract_convert_fusion
  217.3 0.6 pad_maximum_fusion.1
  218.1 0.8 copy-done
  218.9 12.9 %attention.1 = bf16[256,2048]{1,0:T(8,128)(2,1)S(1)} custom-call(s32[2]{0:T(128)S(1)} %copy-done.1, bf16[256,2048]{1,0:T(8,128)(2,1)S(1)} %bitcast.76, bf16[4096,256]{1,0:T(8,128)(2,1)S(1)} %bitcast.75, bf16[4096,256]{1,0:T(8,128)(2,1)S(1)} %bitcast.74), custom_call_target="tpu_custom_call" | custom-call | tf_op jit(solution)/shard_map/attention/pallas_call | solution.py:124
  231.8 51.4 %all-gather.16.cloned.1.call-done = bf16[2048,2048]{0,1:T(8,128)(2,1)} async-done(((bf16[128,2048]{0,1:T(8,128)(2,1)}), bf16[2048,2048]{0,1:T(8,128)(2,1)}) %all-gather.16.cloned.1.call-update) | async-done | bytes 8388624 | tf_op jit(solution)/shard_map/all_gather | solution.py:405
  283.2 5.7 fusion.46
  288.9 1.3 copy-done.6
  290.3 1.6 collective-permute-start
  291.9 12.6 %collective-permute-done = bf16[128,2048]{1,0:T(8,128)(2,1)} collective-permute-done((bf16[128,2048]{1,0:T(8,128)(2,1)S(1)}, bf16[128,2048]{1,0:T(8,128)(2,1)}, u32[]{:S(2)}, u32[]{:S(2)}) %collective-permute-start) | collective-permute-done | bytes 524320 | tf_op jit(solution)/shard_map/ppermute | solution.py:416
  304.5 1.8 multiply_reduce_fusion.1
  306.4 0.9 multiply_convert_fusion
  307.5 54.2 %all-gather.1 = f32[4096,16]{0,1:T(8,128)S(1)} all-gather(f32[128,16]{0,1:T(8,128)S(1)} %pad_maximum_fusion.5), channel_id=3, replica_groups=mesh['ctx'=16,'exp'=2] {'ctx','exp'}, dimensions={0}, use_global_device_ids=true | all-gather | bytes 270336 | tf_op jit(solution)/shard_map/all_gather | solution.py:425
  362.6 0.4 select_reduce_fusion
  363.4 2.0 pad_maximum_fusion
  365.3 0.7 constant_dynamic-slice_fusion
  366.1 56.9 %all-gather.20.cloned.1.call-done = bf16[4096,2048]{1,0:T(8,128)(2,1)} async-done(((bf16[128,2048]{1,0:T(8,128)(2,1)}), bf16[4096,2048]{1,0:T(8,128)(2,1)}) %all-gather.20.cloned.1.call-update) | async-done | bytes 16777232 | tf_op jit(solution)/shard_map/all_gather | solution.py:424
  423.0 11.3 %convolution_convert_fusion.1 = bf16[32,64,2048]{2,1,0:T(8,128)(2,1)} fusion(pred[32,64,128]{2,1,0:T(32,128)(4,1)S(1)} %fusion.23, bf16[32,128,2048]{2,1,0:T(8,128)(2,1)} %bitcast.79), kind=kOutput, calls=%fused_computation.11 | convolution fusion | flops 1077936128 | bytes 25427968 | tf_op jit(solution)/shard_map/ast,atd->asd/dot_general | solution.py:445
  434.3 21.8 %fusion.5 = f32[32,4,16,1536]{3,2,0,1:T(8,128)} fusion(bf16[4,2048,1536]{2,1,0:T(8,128)(2,1)} %param.24, bf16[32,4,16,2048]{3,2,1,0:T(8,128)(2,1)} %bitcast.80), kind=kOutput, calls=%fused_computation.7 | convolution fusion | flops 12884901888 | bytes 46137344 | tf_op jit(solution)/shard_map/arcd,rdf->arcf/dot_general | solution.py:449
  456.1 16.2 %convert_bitcast_fusion = bf16[32,4,16,2048]{3,2,0,1:T(8,128)(2,1)} fusion(bf16[4,768,2048]{2,1,0:T(8,128)(2,1)} %param.25, f32[32,4,16,1536]{3,2,0,1:T(8,128)} %fusion.5, f32[32,4,16]{2,0,1:T(8,128)S(1)} %copy.70), kind=kOutput, calls=%fused_computation.6 | convolution fusion | flops 6457655296 | bytes 33562624 | tf_op jit(solution)/shard_map/arcf,rfd->arcd/dot_general | solution.py:453
  472.3 8.3 %copy.71 = bf16[32,4,16,2048]{3,2,1,0:T(8,128)(2,1)} copy(bf16[32,4,16,2048]{3,2,0,1:T(8,128)(2,1)} %convert_bitcast_fusion) | data formatting | bytes 16777216 | tf_op jit(solution)/shard_map/convert_element_type | solution.py:455
  480.6 13.7 %convolution_convert_fusion = bf16[32,128,2048]{2,1,0:T(8,128)(2,1)} fusion(pred[32,64,128]{2,1,0:T(32,128)(4,1)S(1)} %fusion.23, bf16[32,64,2048]{2,1,0:T(8,128)(2,1)} %bitcast.78), kind=kOutput, calls=%fused_computation.2 | convolution fusion | flops 1082130432 | bytes 25427968 | tf_op jit(solution)/shard_map/ast,asd->atd/dot_general | solution.py:456
  494.2 116.3 %reduce_over_devices.1 = f32[128,2048]{1,0:T(8,128)} custom-call(bf16[4,2,2,2,128,2048]{5,4,3,2,1,0:T(8,128)(2,1)} %bitcast.77), custom_call_target="tpu_custom_call" | custom-call | tf_op jit(solution)/shard_map/reduce_over_devices/pallas_call | solution.py:288
  610.5 2.1 add_convert_fusion.1
  (64 shorter events, 4.3 us)
Async XLA Ops:
  7.2 25.9 %all-gather.10.cloned.1.call-start = ((), (), s32[]{:S(2)}) async-start(), calls=%async_computation | async-start | bytes 1572864 | tf_op jit(solution)/shard_map/all_gather | solution.py:347
  8.4 70.2 %copy-start.11 = (f32[128]{0:T(128)S(1)}, f32[128]{0:T(128)}, u32[]{:S(2)}) copy-start(f32[128]{0:T(128)} %param.21) | copy-start | bytes 1540
  10.5 64.9 %all-gather.14.cloned.1.call-start = ((), (), s32[]{:S(2)}) async-start(), calls=%async_computation.2 | async-start | bytes 2228224 | tf_op jit(solution)/shard_map/all_gather | solution.py:365
  12.2 119.1 %all-gather.18.cloned.1.call-start = ((), (), s32[]{:S(2)}) async-start(), calls=%async_computation.4 | async-start | bytes 4456448 | tf_op jit(solution)/shard_map/all_gather | solution.py:384
  80.7 125.5 %all-gather.12.cloned.1.call-start = ((), (), s32[]{:S(2)}) async-start(), calls=%async_computation.1 | async-start | bytes 8912896 | tf_op jit(solution)/shard_map/all_gather | solution.py:360
  81.2 201.9 %all-gather.16.cloned.1.call-start = ((), (), s32[]{:S(2)}) async-start(), calls=%async_computation.3 | async-start | bytes 8912896 | tf_op jit(solution)/shard_map/all_gather | solution.py:405
  81.8 341.1 %all-gather.20.cloned.1.call-start = ((), (), s32[]{:S(2)}) async-start(), calls=%async_computation.5 | async-start | bytes 17301504 | tf_op jit(solution)/shard_map/all_gather | solution.py:424
  134.7 1.3 copy-start.3
  134.7 2.0 copy-start.5
  136.7 69.4 %copy-start.12 = (bf16[256,2048]{1,0:T(8,128)(2,1)S(1)}, bf16[256,2048]{1,0:T(8,128)(2,1)}, u32[]{:S(2)}) copy-start(bf16[256,2048]{1,0:T(8,128)(2,1)} %all-gather.10.cloned.1.call-done) | copy-start | bytes 3145732
  211.8 2.6 copy-start.10
  212.2 1.4 copy-start.2
  217.3 1.7 copy-start
  217.3 1.6 copy-start.1
  288.9 1.3 copy-start.6
  288.9 17.5 %copy-start.7 = (f32[2048]{0:T(1024)S(1)}, f32[2048]{0:T(1024)}, u32[]{:S(2)}) copy-start(f32[2048]{0:T(1024)} %param.23) | copy-start | bytes 24580
  288.9 18.6 %copy-start.8 = (s32[128,8]{0,1:T(8,128)S(1)}, s32[128,8]{0,1:T(8,128)}, u32[]{:S(2)}) copy-start(s32[128,8]{0,1:T(8,128)} %param.15) | copy-start | bytes 12292
  288.9 18.6 %copy-start.9 = (f32[128,8]{0,1:T(8,128)S(1)}, f32[128,8]{0,1:T(8,128)}, u32[]{:S(2)}) copy-start(f32[128,8]{0,1:T(8,128)} %param.16) | copy-start | bytes 12292
  290.3 14.3 %collective-permute-start = (bf16[128,2048]{1,0:T(8,128)(2,1)S(1)}, bf16[128,2048]{1,0:T(8,128)(2,1)}, u32[]{:S(2)}, u32[]{:S(2)}) collective-permute-start(bf16[128,2048]{1,0:T(8,128)(2,1)S(1)} %fusion.25), channel_id=1, source_target_pairs={{0,1},{1,0},{2,3},{3,2},{4,5},{5,4},{6,7},{7,6},{8,9},{9,8},{10,11... | collective-permute-start | bytes 1572872 | tf_op jit(solution)/shard_map/ppermute | solution.py:416
  291.9 71.5 %copy-start.4 = (bf16[2,16,128,256]{3,2,1,0:T(8,128)(2,1)S(1)}, bf16[2,16,128,256]{3,2,1,0:T(8,128)(2,1)}, u32[]{:S(2)}) copy-start(bf16[2,16,128,256]{3,2,1,0:T(8,128)(2,1)} %copy-done.3) | copy-start | bytes 6291460
Sparse Core Ops, SparseCore 0:
  10.6 22.4 all-gather.9
  35.8 39.5 all-gather.13
  80.8 50.4 all-gather.17
  133.3 72.7 all-gather.11
  208.1 75.0 all-gather.15
  307.5 115.4 all-gather.19

commit v2 on v1

--- a/solution.py
+++ b/solution.py
@@ -344,7 +344,18 @@
     )
     query_doc, query_rope = document_info(query_pos, lengths)
     normed_own = rms_scale(hidden.astype(jnp.float32), attn_gain).astype(jnp.bfloat16)
-    normed = lax.all_gather(normed_own, "exp", axis=0, tiled=True)
+    pieces = [normed_own]
+    for shift in range(1, expert_count):
+        route = [(i, (i + shift) % expert_count) for i in range(expert_count)]
+        pieces.append(lax.ppermute(normed_own, "exp", route))
+    stacked = jnp.stack(pieces)
+    normed = jnp.concatenate(
+        [
+            lax.dynamic_index_in_dim(stacked, (my_exp - j) % expert_count, 0, keepdims=False)
+            for j in range(expert_count)
+        ],
+        axis=0,
+    )
     key_cols = lax.dynamic_slice_in_dim(
         key_value_weight, key_value_leading * HEAD_SIZE, key_value_share * HEAD_SIZE, 1
     )
@@ -355,16 +366,16 @@
         1,
     )
     kv_local = jnp.concatenate([key_cols, value_column_block], axis=1)
-    q_raw = jnp.dot(
-        normed,
-        lax.all_gather(q_weight, "ctx", axis=0, tiled=True),
-        preferred_element_type=jnp.float32,
-    )
-    key_value_plain = jnp.dot(
-        normed,
-        lax.all_gather(kv_local, "ctx", axis=0, tiled=True),
-        preferred_element_type=jnp.float32,
-    )
+    weights = lax.all_gather(
+        jnp.concatenate([q_weight, kv_local, o_weight.T], axis=1), "ctx", axis=0, tiled=True
+    )
+    q_width = q_weight.shape[1]
+    kv_width = kv_local.shape[1]
+    projected = jnp.dot(
+        normed, weights[:, : q_width + kv_width], preferred_element_type=jnp.float32
+    )
+    q_raw = projected[:, :q_width]
+    key_value_plain = projected[:, q_width:]
     queries = rotate(
         rms_scale(q_raw.reshape(tok_ctx, q_dev, HEAD_SIZE), q_gain), query_rope
     ).astype(jnp.bfloat16)
@@ -402,7 +413,7 @@
         key_value_share,
         group_dev,
     )
-    o_rows = lax.all_gather(o_weight.T, "ctx", axis=0, tiled=True)
+    o_rows = weights[:, q_width + kv_width :]
     attn_part = lax.dot_general(
         context, o_rows, (((1,), (1,)), ((), ())), preferred_element_type=jnp.float32
     )

time: 621 us -> 533 us (0.86)
  waiting for transfers between devices: 299 us -> 216 us
    all_gather x4 -> x1, waiting for transfers between devices: 179 us -> 92.3 us  [shards(): lax.all_gather(jnp.concatenate([q_weight, kv_local, o_weight.T], axis=1),...]
    ppermute x0 -> x1, waiting for transfers between devices: none -> 8.8 us  [shards(): pieces.append(lax.ppermute(normed_own, 'exp', route))]
  transfers between devices with their start and end apart: 7 -> 5, of which waited for: 7 -> 5; matrix products, arithmetic and copies ran while one was open for 4% -> 2% of each run, Pallas kernels for 2% -> 0%
where the time goes in v2:
time: 533 us; the launch traced here: 532 us
  waiting for transfers between devices  216 us (41%)
  Pallas kernels  131 us (25%)
  matrix products  74.8 us (14%)
  blocking collectives  51.8 us (10%)
  local copies, waits for them, and re-layouts  19.2 us (4%)
  other arithmetic  19.2 us (4%)
  between operations  15.6 us (3%)
    pallas_call x1, Pallas kernels, reduce_over_devices(): pl.pallas_call(functools.partial(reduce_kernel, Z, E), in_specs=[pl.Block...  116 us
    all_gather x1, waiting for transfers between devices, shards(): lax.all_gather(jnp.concatenate([q_weight, kv_local, o_weight.T], axis=1),...  92.3 us
    all_gather x1, waiting for transfers between devices, shards(): tokens = lax.all_gather(moe_in, ('ctx', 'exp'), axis=0)  57.7 us
    all_gather x1, blocking collectives, shards(): lax.all_gather(jnp.concatenate([routes.astype(jnp.float32), gates], axis=...  51.8 us
    all_gather x1, waiting for transfers between devices, shards(): gathered = lax.all_gather(key_values, 'ctx', axis=0)  44.8 us
    dot_general x1, matrix products, shards(): jnp.einsum('arcd,rdf->arcf', arrived, expert_in, preferred_element_type=j...  21.7 us
    dot_general x1, matrix products, shards(): jnp.einsum('arcf,rfd->arcd', activated, expert_out, preferred_element_typ...  16.2 us
    pallas_call x1, Pallas kernels, attention(): pl.pallas_call(functools.partial(attention_kernel, count_ctx, half_rows,...  15.1 us
  transfers between devices with their start and end apart: 5, of which 5 were waited for; matrix products, arithmetic and copies ran while one was open for 2% of the time, Pallas kernels for 0%

profile of v2, /device:TPU:10, one launch (start us, length us, event | category | flops | bytes accessed | tf_op | source)
XLA Modules:
  0.0 531.8 jit_solution(16035961987465090051)
XLA Ops:
  7.2 0.9 constant_dynamic-slice_fusion.2
  8.4 1.3 copy.76
  9.8 2.1 pad_maximum_fusion.1
  12.4 1.6 collective-permute-start
  14.0 0.6 fusion.56
  15.9 0.7 fusion.48
  16.5 0.5 multiply_cosine_fusion
  17.3 8.8 %collective-permute-done = bf16[128,2048]{1,0:T(8,128)(2,1)S(1)} collective-permute-done((bf16[128,2048]{1,0:T(8,128)(2,1)S(1)}, bf16[128,2048]{1,0:T(8,128)(2,1)S(1)}, u32[]{:S(2)}, u32[]{:S(2)}) %collective-permute-start) | collective-permute-done | bytes 524320 | tf_op jit(solution)/shard_map/ppermute | solution.py:350
  26.1 1.4 fusion.36
  27.5 92.3 %all-gather.7.cloned.1.call-done = bf16[2048,4608]{0,1:T(8,128)(2,1)} async-done(((bf16[128,4608]{0,1:T(8,128)(2,1)}), bf16[2048,4608]{0,1:T(8,128)(2,1)}) %all-gather.7.cloned.1.call-update) | async-done | bytes 18874384 | tf_op jit(solution)/shard_map/all_gather | solution.py:369
  119.8 6.0 %fusion.4 = f32[256,2560]{1,0:T(8,128)S(1)} fusion(bf16[2048,4608]{0,1:T(8,128)(2,1)} %all-gather.7.cloned.1.call-done, bf16[128,2048]{1,0:T(8,128)(2,1)} %get-tuple-element.11, bf16[128,2048]{1,0:T(8,128)(2,1)} %get-tuple-element.10), kind=kOutput, calls=%fused_computation.5 | convolution fusion | flops 2686451712 | bytes 14155776 | tf_op jit(solution)/shard_map/dot_general | solution.py:374
  126.0 0.3 multiply_reduce_fusion.2
  126.3 0.3 multiply_multiply_fusion.1
  126.7 0.5 subtract_convert_fusion.1
  127.2 0.4 pad_maximum_fusion.4
  127.7 0.7 pad_maximum_fusion.3
  128.9 0.4 copy.98
  129.2 0.6 multiply_reduce_fusion
  130.1 0.9 multiply_multiply_fusion
  130.9 0.8 subtract_convert_fusion
  131.8 0.6 pad_maximum_fusion.2
  132.4 0.3 copy.111
  132.6 44.8 %all-gather.9.cloned.1.call-done = bf16[32,256,256]{2,1,0:T(8,128)(2,1)} async-done(((bf16[2,256,256]{2,1,0:T(8,128)(2,1)}), bf16[32,256,256]{2,1,0:T(8,128)(2,1)}) %all-gather.9.cloned.1.call-update) | async-done | bytes 4194320 | tf_op jit(solution)/shard_map/all_gather | solution.py:395
  177.5 2.7 fusion.54
  180.4 0.4 copy_bitcast_fusion
  180.8 0.4 fusion.22
  181.2 0.9 copy-done.1
  182.1 15.1 %attention.1 = bf16[256,2048]{1,0:T(8,128)(2,1)S(1)} custom-call(s32[2]{0:T(128)S(1)} %copy-done, bf16[256,2048]{1,0:T(8,128)(2,1)S(1)} %bitcast.78, bf16[4096,256]{1,0:T(8,128)(2,1)S(1)} %bitcast.77, bf16[4096,256]{1,0:T(8,128)(2,1)S(1)} %bitcast.76), custom_call_target="tpu_custom_call" | custom-call | tf_op jit(solution)/shard_map/attention/pallas_call | solution.py:124
  197.2 5.8 %fusion.6 = f32[256,2048]{1,0:T(8,128)S(1)} fusion(bf16[256,2048]{1,0:T(8,128)(2,1)S(1)} %attention.1, bf16[2048,4608]{0,1:T(8,128)(2,1)} %all-gather.7.cloned.1.call-done), kind=kOutput, calls=%fused_computation.7 | convolution fusion | flops 2147483648 | bytes 11534336 | tf_op jit(solution)/shard_map/dot_general | solution.py:417
  203.0 1.3 copy-done.3
  204.4 1.5 collective-permute-start.1
  205.9 12.7 %collective-permute-done.1 = bf16[128,2048]{1,0:T(8,128)(2,1)} collective-permute-done((bf16[128,2048]{1,0:T(8,128)(2,1)S(1)}, bf16[128,2048]{1,0:T(8,128)(2,1)}, u32[]{:S(2)}, u32[]{:S(2)}) %collective-permute-start.1) | collective-permute-done | bytes 524320 | tf_op jit(solution)/shard_map/ppermute | solution.py:427
  218.6 1.8 multiply_reduce_fusion.1
  220.5 0.9 multiply_convert_fusion
  221.6 51.8 %all-gather.1 = f32[4096,16]{0,1:T(8,128)S(1)} all-gather(f32[128,16]{0,1:T(8,128)S(1)} %pad_maximum_fusion.5), channel_id=3, replica_groups=mesh['ctx'=16,'exp'=2] {'ctx','exp'}, dimensions={0}, use_global_device_ids=true | all-gather | bytes 270336 | tf_op jit(solution)/shard_map/all_gather | solution.py:436
  274.1 0.3 fusion.31
  274.3 0.4 select_reduce_fusion
  274.8 0.3 fusion.30
  275.1 2.0 pad_maximum_fusion
  277.0 0.7 constant_dynamic-slice_fusion
  277.7 57.7 %all-gather.11.cloned.1.call-done = bf16[4096,2048]{1,0:T(8,128)(2,1)} async-done(((bf16[128,2048]{1,0:T(8,128)(2,1)}), bf16[4096,2048]{1,0:T(8,128)(2,1)}) %all-gather.11.cloned.1.call-update) | async-done | bytes 16777232 | tf_op jit(solution)/shard_map/all_gather | solution.py:435
  335.5 11.3 %convolution_convert_fusion.1 = bf16[32,64,2048]{2,1,0:T(8,128)(2,1)} fusion(pred[32,64,128]{2,1,0:T(32,128)(4,1)S(1)} %fusion.30, bf16[32,128,2048]{2,1,0:T(8,128)(2,1)} %bitcast.81), kind=kOutput, calls=%fused_computation.15 | convolution fusion | flops 1077936128 | bytes 25427968 | tf_op jit(solution)/shard_map/ast,atd->asd/dot_general | solution.py:456
  346.8 21.7 %fusion.9 = f32[32,4,16,1536]{3,2,0,1:T(8,128)} fusion(bf16[4,2048,1536]{2,1,0:T(8,128)(2,1)} %param.24, bf16[32,4,16,2048]{3,2,1,0:T(8,128)(2,1)} %bitcast.82), kind=kOutput, calls=%fused_computation.11 | convolution fusion | flops 12884901888 | bytes 46137344 | tf_op jit(solution)/shard_map/arcd,rdf->arcf/dot_general | solution.py:460
  368.5 16.2 %convert_bitcast_fusion = bf16[32,4,16,2048]{3,2,0,1:T(8,128)(2,1)} fusion(bf16[4,768,2048]{2,1,0:T(8,128)(2,1)} %param.25, f32[32,4,16,1536]{3,2,0,1:T(8,128)} %fusion.9, f32[32,4,16]{2,0,1:T(8,128)S(1)} %copy.88), kind=kOutput, calls=%fused_computation.10 | convolution fusion | flops 6457655296 | bytes 33562624 | tf_op jit(solution)/shard_map/arcf,rfd->arcd/dot_general | solution.py:464
  384.8 8.3 %copy.89 = bf16[32,4,16,2048]{3,2,1,0:T(8,128)(2,1)} copy(bf16[32,4,16,2048]{3,2,0,1:T(8,128)(2,1)} %convert_bitcast_fusion) | data formatting | bytes 16777216 | tf_op jit(solution)/shard_map/convert_element_type | solution.py:466
  393.1 13.7 %convolution_convert_fusion = bf16[32,128,2048]{2,1,0:T(8,128)(2,1)} fusion(pred[32,64,128]{2,1,0:T(32,128)(4,1)S(1)} %fusion.30, bf16[32,64,2048]{2,1,0:T(8,128)(2,1)} %bitcast.80), kind=kOutput, calls=%fused_computation.2 | convolution fusion | flops 1082130432 | bytes 25427968 | tf_op jit(solution)/shard_map/ast,asd->atd/dot_general | solution.py:467
  406.8 116.3 %reduce_over_devices.1 = f32[128,2048]{1,0:T(8,128)} custom-call(bf16[4,2,2,2,128,2048]{5,4,3,2,1,0:T(8,128)(2,1)} %bitcast.79), custom_call_target="tpu_custom_call" | custom-call | tf_op jit(solution)/shard_map/reduce_over_devices/pallas_call | solution.py:288
  523.1 2.2 add_convert_fusion.1
  (56 shorter events, 2.9 us)
Async XLA Ops:
  7.2 4.8 copy-start.2
  7.2 112.6 %all-gather.7.cloned.1.call-start = ((), (), s32[]{:S(2)}) async-start(), calls=%async_computation | async-start | bytes 20054016 | tf_op jit(solution)/shard_map/all_gather | solution.py:369
  8.3 3.9 copy-start.4
  9.8 4.2 copy-start
  11.9 165.6 %all-gather.9.cloned.1.call-start = ((), (), s32[]{:S(2)}) async-start(), calls=%async_computation.1 | async-start | bytes 4456448 | tf_op jit(solution)/shard_map/all_gather | solution.py:395
  12.4 13.7 %collective-permute-start = (bf16[128,2048]{1,0:T(8,128)(2,1)S(1)}, bf16[128,2048]{1,0:T(8,128)(2,1)S(1)}, u32[]{:S(2)}, u32[]{:S(2)}) collective-permute-start(bf16[128,2048]{1,0:T(8,128)(2,1)S(1)} %fusion.25), channel_id=1, source_target_pairs={{0,1},{1,0},{2,3},{3,2},{4,5},{5,4},{6,7},{7,6},{8,9},{9,8},{10,11... | collective-permute-start | bytes 1572872 | tf_op jit(solution)/shard_map/ppermute | solution.py:350
  119.8 6.6 %copy-start.9 = (f32[128]{0:T(128)S(1)}, f32[128]{0:T(128)}, u32[]{:S(2)}) copy-start(f32[128]{0:T(128)} %param.21) | copy-start | bytes 1540
  128.4 207.0 %all-gather.11.cloned.1.call-start = ((), (), s32[]{:S(2)}) async-start(), calls=%async_computation.2 | async-start | bytes 17301504 | tf_op jit(solution)/shard_map/all_gather | solution.py:435
  128.8 1.2 copy-start.8
  180.8 1.3 copy-start.1
  203.0 1.3 copy-start.3
  203.0 17.5 %copy-start.5 = (f32[2048]{0:T(1024)S(1)}, f32[2048]{0:T(1024)}, u32[]{:S(2)}) copy-start(f32[2048]{0:T(1024)} %param.23) | copy-start | bytes 24580
  204.4 14.3 %collective-permute-start.1 = (bf16[128,2048]{1,0:T(8,128)(2,1)S(1)}, bf16[128,2048]{1,0:T(8,128)(2,1)}, u32[]{:S(2)}, u32[]{:S(2)}) collective-permute-start(bf16[128,2048]{1,0:T(8,128)(2,1)S(1)} %fusion.32), channel_id=1, source_target_pairs={{0,1},{1,0},{2,3},{3,2},{4,5},{5,4},{6,7},{7,6},{8,9},{9,8},{10,11... | collective-permute-start | bytes 1572872 | tf_op jit(solution)/shard_map/ppermute | solution.py:427
  205.9 15.7 %copy-start.6 = (s32[128,8]{0,1:T(8,128)S(1)}, s32[128,8]{0,1:T(8,128)}, u32[]{:S(2)}) copy-start(s32[128,8]{0,1:T(8,128)} %param.15) | copy-start | bytes 12292
  205.9 15.7 %copy-start.7 = (f32[128,8]{0,1:T(8,128)S(1)}, f32[128,8]{0,1:T(8,128)}, u32[]{:S(2)}) copy-start(f32[128,8]{0,1:T(8,128)} %param.16) | copy-start | bytes 12292
Sparse Core Ops, SparseCore 0:
  12.0 107.6 all-gather.6
  128.5 48.9 all-gather.8
  221.6 113.8 all-gather.10
